TPU v7x, 32 devices: a whole 2x2x4 slice. The times are simulated.
32 devices in a mesh: region: 8 (over z, x), tm: 4 (over y, core).
Axes of the slice: x: 2, y: 2, z: 4, core: 2. Of those that a mesh axis runs over, the one named last changes fastest.
Arguments:
- right_side: float32 [1024, 4096], P('tm', 'region'), may hold values from -9 to 9
- initial: float32 [1024, 4096], P('tm', 'region'), may hold values from -1.5 to 1.5
- blocks: bfloat16 [32, 9, 128, 128], P(('region', 'tm')), may hold values from -2.5 to 3.1, as said below
- neighbour_blocks: int32 [32, 8], P('region'), may hold values from 0 to 31, as said below
- temporal_cov: bfloat16 [1024, 1024], P('tm'), may hold values from -2.5 to 2.8, as said below
Outputs:
- solution: float32 [1024, 4096], P('tm', 'region')
- residual: float32 [1024, 4096], P('tm', 'region')
Inputs may be any that keep to these rules, and one draw needn't show every extreme that they name: blocks[i, 0] is symmetric positive definite. `neighbour_blocks`: each column names every block exactly once. Blocks fall into cyclic windows of 4 consecutive blocks starting at 2 + m * 4, and every block listed for row i lies in the window of i. temporal_cov is symmetric positive definite.
All inputs are finite; a program needn't handle non-finite values.
Results may differ from a plain program's by a relative error of at most 0.012.
The roundings to bfloat16 on the way count: a program that leaves them out, or rounds other values in their place, can miss the bound.
Values may be sent and summed in bfloat16 or wider, within the bound.
A program may use at most 64 MiB of HBM per device.

v0:
```python
import functools

import jax
import jax.numpy as jnp
from jax import lax
from jax.experimental import pallas as pl
from jax.experimental.pallas import tpu as pltpu
from jax.sharding import PartitionSpec as P

ITERS = 2
CORES = 2
MESH = pl.DeviceIdType.MESH
NT = (((1,), (1,)), ((), ()))


def fold(value):
    height, width = value.shape
    tall = jnp.sum(value.reshape(height // 8, 8, width), axis=0)
    total = tall[:, :128]
    for lane in range(128, width, 128):
        total = total + tall[:, lane : lane + 128]
    return total


def total_of(value):
    return jnp.sum(jnp.sum(value, axis=1, keepdims=True), axis=0, keepdims=True)


def kernel(
    regions,
    peers,
    right_ref,
    initial_ref,
    blocks_ref,
    places_ref,
    cov_ref,
    solution_ref,
    residual_ref,
    matrix,
    wide,
    gathered,
    direction,
    image,
    near,
    far,
    halo_send,
    halo_recv,
    matrix_send,
    matrix_recv,
    field_send,
    field_recv,
    near_send,
    near_recv,
    far_send,
    far_recv,
):
    hours, sites = right_ref.shape
    own_rows, slots, tile, _ = blocks_ref.shape
    rows = places_ref.shape[0]
    half = rows // 2
    edge = half * tile
    chips = peers // CORES
    region = lax.axis_index("region")
    peer = lax.axis_index("tm")
    chip = peer // CORES
    core = peer % CORES
    sibling = chip * CORES + (CORES - 1 - core)
    pending = []

    def region_at(step):
        return lax.rem(region + step + regions, regions)

    def peer_at(step):
        return lax.rem(peer + step + peers, peers)

    barrier = pltpu.get_barrier_semaphore()
    for step in range(1, peers):
        pl.semaphore_signal(
            barrier, inc=1, device_id=(region, peer_at(step)), device_id_type=MESH
        )
    for step in range(1, regions):
        pl.semaphore_signal(
            barrier, inc=1, device_id=(region_at(step), peer), device_id_type=MESH
        )

    def copy(source, target, send, recv, device):
        return pltpu.make_async_remote_copy(
            src_ref=source,
            dst_ref=target,
            send_sem=send,
            recv_sem=recv,
            device_id=device,
            device_id_type=MESH,
        )

    def start(*parts):
        made = copy(*parts)
        made.start()
        pending.append(made)

    def await_into(target, send, recv):
        copy(target, target, send, recv, (region, sibling)).wait_recv()

    def rows_of(index, size):
        return pl.ds(pl.multiple_of(index * size, size), size)

    class Gather:
        def __init__(self, view, send, recv):
            self.view, self.send, self.recv = view, send, recv

        def begin(self):
            own = self.view(peer)
            for step in range(1, chips):
                other = lax.rem(chip + step, chips) * CORES + core
                start(own, own, self.send.at[step], self.recv.at[step], (region, other))
            start(own, own, self.send.at[0], self.recv.at[0], (region, sibling))

        def forward(self):
            for step in range(1, chips):
                other = lax.rem(chip - step + chips, chips) * CORES + core
                part = self.view(other)
                await_into(part, self.send.at[step], self.recv.at[step])
                place = chips - 1 + step
                start(part, part, self.send.at[place], self.recv.at[place], (region, sibling))

        def finish(self):
            await_into(self.view(sibling), self.send.at[0], self.recv.at[0])
            for step in range(1, chips):
                other = lax.rem(chip - step + chips, chips) * CORES + (CORES - 1 - core)
                place = chips - 1 + step
                await_into(self.view(other), self.send.at[place], self.recv.at[place])

    def send_halo(turn, value):
        field = wide.at[turn]
        field[:, edge : edge + sites] = value.astype(jnp.bfloat16)
        if turn == 0:
            pl.semaphore_wait(barrier, peers + regions - 2)
        start(
            field.at[:, sites : sites + edge],
            field.at[:, 0:edge],
            halo_send.at[turn, 0],
            halo_recv.at[turn, 0],
            (region_at(1), peer),
        )
        start(
            field.at[:, edge : 2 * edge],
            field.at[:, edge + sites : 2 * edge + sites],
            halo_send.at[turn, 1],
            halo_recv.at[turn, 1],
            (region_at(-1), peer),
        )

    matrix_gather = Gather(
        lambda index: matrix.at[rows_of(index, own_rows * tile), :], matrix_send, matrix_recv
    )

    def build_matrix():
        for own in range(own_rows):
            row = peer * own_rows + own
            shift = jnp.where(row < half, -half, half)
            base = region * rows + shift
            spots = [row - shift]
            for slot in range(slots - 1):
                spots.append(lax.rem(places_ref[row, slot] - base + regions * rows, regions * rows))
            for column in range(rows):
                total = jnp.zeros((tile, tile), jnp.float32)
                for slot in range(slots):
                    weight = jnp.where(spots[slot] == column, 1.0, 0.0).astype(jnp.float32)
                    total = total + weight * blocks_ref[own, slot].astype(jnp.float32)
                matrix[rows_of(row, tile), column * tile : (column + 1) * tile] = total.astype(
                    jnp.bfloat16
                )
        matrix_gather.begin()

    def operate(turn):
        if turn == 0:
            build_matrix()
            matrix_gather.forward()
            matrix_gather.finish()
        field = wide.at[turn]
        gathers = []
        for side in range(2):
            landed = field.at[:, 0:edge] if side == 0 else field.at[:, edge + sites : 2 * edge + sites]
            await_into(landed, halo_send.at[turn, side], halo_recv.at[turn, side])
            spatial = lax.dot_general(
                field[:, side * sites : (side + 1) * sites],
                matrix[side * edge : (side + 1) * edge, :],
                NT,
                preferred_element_type=jnp.float32,
            )
            columns = slice(side * edge, (side + 1) * edge)
            gathered[turn, rows_of(peer, hours), columns] = spatial.astype(jnp.bfloat16)
            gather = Gather(
                lambda index, columns=columns: gathered.at[turn, rows_of(index, hours), columns],
                field_send.at[turn, side],
                field_recv.at[turn, side],
            )
            gather.begin()
            gathers.append(gather)
        for gather in gathers:
            gather.forward()
        for side, gather in enumerate(gathers):
            gather.finish()
            columns = slice(side * edge, (side + 1) * edge)
            temporal = jnp.dot(
                cov_ref[...], gathered[turn, :, columns], preferred_element_type=jnp.float32
            )
            yield columns, temporal.astype(jnp.bfloat16).astype(jnp.float32)

    def reduce(turn, parts):
        count = len(parts) * 8
        for place, part in enumerate(parts):
            near[turn, peer, place * 8 : (place + 1) * 8, :] = part
        own = near.at[turn, peer, 0:count]
        for step in range(1, peers):
            start(own, own, near_send.at[turn, step], near_recv.at[turn, step], (region, peer_at(step)))
        for step in range(1, peers):
            await_into(
                near.at[turn, peer_at(-step), 0:count],
                near_send.at[turn, step],
                near_recv.at[turn, step],
            )
        far[turn, region, 0:count, :] = jnp.sum(near[turn, :, 0:count, :], axis=0)
        own = far.at[turn, region, 0:count]
        for step in range(1, regions):
            start(own, own, far_send.at[turn, step], far_recv.at[turn, step], (region_at(step), peer))
        for step in range(1, regions):
            await_into(
                far.at[turn, region_at(-step), 0:count],
                far_send.at[turn, step],
                far_recv.at[turn, step],
            )
        whole = jnp.sum(far[turn, :, 0:count, :], axis=0)
        return [total_of(whole[place * 8 : (place + 1) * 8]) for place in range(len(parts))]

    send_halo(0, initial_ref[...])
    for columns, temporal in operate(0):
        direction[:, columns] = right_ref[:, columns] - (initial_ref[:, columns] + temporal)
    residual_ref[...] = direction[...]
    solution_ref[...] = initial_ref[...]
    norm = None
    for turn in range(ITERS):
        send_halo(turn + 1, direction[...])
        for columns, temporal in operate(turn + 1):
            image[:, columns] = direction[:, columns] + temporal
        parts = [fold(direction[...] * image[...])]
        if turn + 1 < ITERS:
            parts.append(fold(residual_ref[...] * image[...]))
            parts.append(fold(image[...] * image[...]))
        if turn == 0:
            parts.append(fold(residual_ref[...] * residual_ref[...]))
        sums = reduce(turn, parts)
        if turn == 0:
            norm = sums[-1]
        step_size = norm / sums[0]
        solution_ref[...] = solution_ref[...] + step_size * direction[...]
        residual_ref[...] = residual_ref[...] - step_size * image[...]
        if turn + 1 < ITERS:
            later = norm - 2.0 * step_size * sums[1] + step_size * step_size * sums[2]
            direction[...] = residual_ref[...] + later / norm * direction[...]
            norm = later
    for made in pending:
        made.wait_send()


def local(regions, peers, right_side, initial, blocks, neighbour_blocks, temporal_cov):
    hours, sites = right_side.shape
    rows = neighbour_blocks.shape[0]
    tile = blocks.shape[2]
    turns = ITERS + 1
    dma = pltpu.SemaphoreType.DMA
    vmem = pl.BlockSpec(memory_space=pltpu.VMEM)
    out = jax.ShapeDtypeStruct((hours, sites), jnp.float32)
    width = 2 * sites
    flops = turns * 2 * hours * sites * (rows * tile + temporal_cov.shape[1])
    return pl.pallas_call(
        functools.partial(kernel, regions, peers),
        out_shape=(out, out),
        in_specs=[vmem, vmem, vmem, pl.BlockSpec(memory_space=pltpu.SMEM), vmem],
        out_specs=(vmem, vmem),
        scratch_shapes=[
            pltpu.VMEM((rows * tile, rows * tile), jnp.bfloat16),
            pltpu.VMEM((turns, hours, width), jnp.bfloat16),
            pltpu.VMEM((turns, hours * peers, sites), jnp.bfloat16),
            pltpu.VMEM((hours, sites), jnp.float32),
            pltpu.VMEM((hours, sites), jnp.float32),
            pltpu.VMEM((ITERS, peers, 32, 128), jnp.float32),
            pltpu.VMEM((ITERS, regions, 32, 128), jnp.float32),
            dma((turns, 2)),
            dma((turns, 2)),
            dma((peers - 1,)),
            dma((peers - 1,)),
            dma((turns, 2, peers - 1)),
            dma((turns, 2, peers - 1)),
            dma((ITERS, peers)),
            dma((ITERS, peers)),
            dma((ITERS, regions)),
            dma((ITERS, regions)),
        ],
        compiler_params=pltpu.CompilerParams(
            collective_id=0, has_side_effects=True, vmem_limit_bytes=56 * 1024 * 1024
        ),
        cost_estimate=pl.CostEstimate(flops=flops, bytes_accessed=4 * hours * width, transcendentals=0),
    )(right_side, initial, blocks, neighbour_blocks, temporal_cov)


def solution(mesh):
    in_specs = (
        P("tm", "region"),
        P("tm", "region"),
        P(("region", "tm"), None, None, None),
        P("region", None),
        P("tm", None),
    )
    out_specs = (P("tm", "region"), P("tm", "region"))
    body = functools.partial(local, mesh.shape["region"], mesh.shape["tm"])
    return jax.shard_map(body, mesh=mesh, in_specs=in_specs, out_specs=out_specs, check_vma=False)
```

profile of v0, /device:TPU:0, one launch (start us, length us, event | category | flops | bytes accessed | tf_op | source)
XLA Modules:
  0.0 73.6 jit_solution(3893235010587790003)
XLA Ops:
  0.6 70.3 %shard_map.68 = (f32[256,512]{1,0:T(8,128)}, f32[256,512]{1,0:T(8,128)}) custom-call(f32[256,512]{1,0:T(8,128)} %right_ref.1, f32[256,512]{1,0:T(8,128)} %initial_ref.1, bf16[1,9,128,128]{3,2,1,0:T(8,128)(2,1)} %blocks_ref.1, s32[4,8]{1,0:T(4,128)} %places_ref.1, bf16[256,1024]{1,0:T(8,128)(2,1)} %cov_ref.1), custom_call_target="tpu_custom_call" | custom-call | flops 1207959552 | bytes 1048576 | tf_op jit(solution)/shard_map/pallas_call | solution.py:276
  70.9 0.0 copy-start
  70.9 1.9 %copy.9 = f32[256,512]{1,0:T(8,128)} copy(f32[256,512]{1,0:T(8,128)} %get-tuple-element.4) | data formatting | bytes 1048576
  72.8 0.0 copy-done
  72.8 0.8 %copy.10 = f32[256,512]{1,0:T(8,128)} copy(f32[256,512]{1,0:T(8,128)S(1)} %copy-done) | data formatting | bytes 1048576
Async XLA Ops:
  70.9 1.9 %copy-start = (f32[256,512]{1,0:T(8,128)S(1)}, f32[256,512]{1,0:T(8,128)}, u32[]{:S(2)}) copy-start(f32[256,512]{1,0:T(8,128)} %get-tuple-element.5) | copy-start | bytes 1572868
where the time goes:
time: 73.8 us; the launch traced here: 73.6 us
  Pallas kernels  70.3 us (95%)
  local copies, waits for them, and re-layouts  2.72 us (4%)
    pallas_call x1, Pallas kernels, local(): pl.pallas_call(functools.partial(kernel, regions, peers), out_shape=(out,...  70.3 us
    unnamed x4, local copies, waits for them, and re-layouts  2.72 us

commit v1 on v0

--- a/solution.py
+++ b/solution.py
@@ -132,26 +132,28 @@
 
     def send_halo(turn, value):
         field = wide.at[turn]
-        field[:, edge : edge + sites] = value.astype(jnp.bfloat16)
+        field[1] = value[:, 0:edge].astype(jnp.bfloat16)
+        field[2] = value[:, edge:sites].astype(jnp.bfloat16)
         if turn == 0:
             pl.semaphore_wait(barrier, peers + regions - 2)
+            matrix_gather.begin()
         start(
-            field.at[:, sites : sites + edge],
-            field.at[:, 0:edge],
+            field.at[2],
+            field.at[0],
             halo_send.at[turn, 0],
             halo_recv.at[turn, 0],
             (region_at(1), peer),
         )
         start(
-            field.at[:, edge : 2 * edge],
-            field.at[:, edge + sites : 2 * edge + sites],
+            field.at[1],
+            field.at[3],
             halo_send.at[turn, 1],
             halo_recv.at[turn, 1],
             (region_at(-1), peer),
         )
 
     matrix_gather = Gather(
-        lambda index: matrix.at[rows_of(index, own_rows * tile), :], matrix_send, matrix_recv
+        lambda index: matrix.at[pl.ds(index * own_rows, own_rows)], matrix_send, matrix_recv
     )
 
     def build_matrix():
@@ -167,31 +169,36 @@
                 for slot in range(slots):
                     weight = jnp.where(spots[slot] == column, 1.0, 0.0).astype(jnp.float32)
                     total = total + weight * blocks_ref[own, slot].astype(jnp.float32)
-                matrix[rows_of(row, tile), column * tile : (column + 1) * tile] = total.astype(
-                    jnp.bfloat16
-                )
-        matrix_gather.begin()
+                high = total.astype(jnp.bfloat16)
+                low = (total - high.astype(jnp.float32)).astype(jnp.bfloat16)
+                across = slice(column * tile, (column + 1) * tile)
+                matrix[row, 0, :, across] = high
+                matrix[row, 1, :, across] = low
 
     def operate(turn):
         if turn == 0:
-            build_matrix()
             matrix_gather.forward()
             matrix_gather.finish()
         field = wide.at[turn]
         gathers = []
         for side in range(2):
-            landed = field.at[:, 0:edge] if side == 0 else field.at[:, edge + sites : 2 * edge + sites]
+            landed = field.at[3 * side]
             await_into(landed, halo_send.at[turn, side], halo_recv.at[turn, side])
-            spatial = lax.dot_general(
-                field[:, side * sites : (side + 1) * sites],
-                matrix[side * edge : (side + 1) * edge, :],
-                NT,
-                preferred_element_type=jnp.float32,
-            )
-            columns = slice(side * edge, (side + 1) * edge)
-            gathered[turn, rows_of(peer, hours), columns] = spatial.astype(jnp.bfloat16)
+            spatial = jnp.zeros((hours, edge), jnp.float32)
+            for level in range(2):
+                for piece in range(2):
+                    part = matrix[
+                        side * half : (side + 1) * half, level, :, piece * edge : (piece + 1) * edge
+                    ]
+                    spatial = spatial + lax.dot_general(
+                        field[2 * side + piece],
+                        part.reshape(edge, edge),
+                        NT,
+                        preferred_element_type=jnp.float32,
+                    )
+            gathered[turn, side, rows_of(peer, hours)] = spatial.astype(jnp.bfloat16)
             gather = Gather(
-                lambda index, columns=columns: gathered.at[turn, rows_of(index, hours), columns],
+                lambda index, side=side: gathered.at[turn, side, rows_of(index, hours)],
                 field_send.at[turn, side],
                 field_recv.at[turn, side],
             )
@@ -203,7 +210,7 @@
             gather.finish()
             columns = slice(side * edge, (side + 1) * edge)
             temporal = jnp.dot(
-                cov_ref[...], gathered[turn, :, columns], preferred_element_type=jnp.float32
+                cov_ref[...], gathered[turn, side], preferred_element_type=jnp.float32
             )
             yield columns, temporal.astype(jnp.bfloat16).astype(jnp.float32)
 
@@ -233,6 +240,7 @@
         whole = jnp.sum(far[turn, :, 0:count, :], axis=0)
         return [total_of(whole[place * 8 : (place + 1) * 8]) for place in range(len(parts))]
 
+    build_matrix()
     send_halo(0, initial_ref[...])
     for columns, temporal in operate(0):
         direction[:, columns] = right_ref[:, columns] - (initial_ref[:, columns] + temporal)
@@ -272,6 +280,7 @@
     vmem = pl.BlockSpec(memory_space=pltpu.VMEM)
     out = jax.ShapeDtypeStruct((hours, sites), jnp.float32)
     width = 2 * sites
+    held = 4 * (rows * tile) ** 2 + 4 * turns * sites * hours * (peers // 2 + 1) + 24 * hours * sites
     flops = turns * 2 * hours * sites * (rows * tile + temporal_cov.shape[1])
     return pl.pallas_call(
         functools.partial(kernel, regions, peers),
@@ -279,9 +288,9 @@
         in_specs=[vmem, vmem, vmem, pl.BlockSpec(memory_space=pltpu.SMEM), vmem],
         out_specs=(vmem, vmem),
         scratch_shapes=[
-            pltpu.VMEM((rows * tile, rows * tile), jnp.bfloat16),
-            pltpu.VMEM((turns, hours, width), jnp.bfloat16),
-            pltpu.VMEM((turns, hours * peers, sites), jnp.bfloat16),
+            pltpu.VMEM((rows, 2, tile, rows * tile), jnp.bfloat16),
+            pltpu.VMEM((turns, 4, hours, sites // 2), jnp.bfloat16),
+            pltpu.VMEM((turns, 2, hours * peers, sites // 2), jnp.bfloat16),
             pltpu.VMEM((hours, sites), jnp.float32),
             pltpu.VMEM((hours, sites), jnp.float32),
             pltpu.VMEM((ITERS, peers, 32, 128), jnp.float32),
@@ -298,7 +307,7 @@
             dma((ITERS, regions)),
         ],
         compiler_params=pltpu.CompilerParams(
-            collective_id=0, has_side_effects=True, vmem_limit_bytes=56 * 1024 * 1024
+            collective_id=0, has_side_effects=True, vmem_limit_bytes=min(3 * held, 58 << 20)
         ),
         cost_estimate=pl.CostEstimate(flops=flops, bytes_accessed=4 * hours * width, transcendentals=0),
     )(right_side, initial, blocks, neighbour_blocks, temporal_cov)

time: 73.8 us -> 78.4 us (1.062)
  local copies, waits for them, and re-layouts: 2.72 us -> 6.35 us
  Pallas kernels: 70.3 us -> 71.1 us
    unnamed x4 -> x12, local copies, waits for them, and re-layouts: 2.72 us -> 6.35 us
    pallas_call x1, Pallas kernels: 70.3 us -> 71.1 us  [local(): pl.pallas_call(functools.partial(kernel, regions, peers), out_shape=(out,...]
where the time goes in v1:
time: 78.4 us; the launch traced here: 78.1 us
  Pallas kernels  71.1 us (91%)
  local copies, waits for them, and re-layouts  6.35 us (8%)
    pallas_call x1, Pallas kernels, local(): pl.pallas_call(functools.partial(kernel, regions, peers), out_shape=(out,...  71.1 us
    unnamed x12, local copies, waits for them, and re-layouts  6.35 us

profile of v1, /device:TPU:0, one launch (start us, length us, event | category | flops | bytes accessed | tf_op | source)
XLA Modules:
  0.0 78.1 jit_solution(16133108353492548990)
XLA Ops:
  0.6 0.0 copy-start
  0.6 1.0 %copy-done = f32[256,512]{1,0:T(8,128)S(1)} copy-done((f32[256,512]{1,0:T(8,128)S(1)}, f32[256,512]{1,0:T(8,128)}, u32[]{:S(2)}) %copy-start) | copy-done | bytes 524312
  1.7 0.0 copy-start.1
  1.7 1.0 %copy-done.1 = f32[256,512]{1,0:T(8,128)S(1)} copy-done((f32[256,512]{1,0:T(8,128)S(1)}, f32[256,512]{1,0:T(8,128)}, u32[]{:S(2)}) %copy-start.1) | copy-done | bytes 524312
  2.7 0.0 copy-start.2
  2.7 1.0 %copy-done.2 = bf16[256,1024]{1,0:T(8,128)(2,1)S(1)} copy-done((bf16[256,1024]{1,0:T(8,128)(2,1)S(1)}, bf16[256,1024]{1,0:T(8,128)(2,1)}, u32[]{:S(2)}) %copy-start.2) | copy-done | bytes 524312
  3.8 0.0 copy-start.3
  3.8 1.0 %copy-done.3 = bf16[1,9,128,128]{3,2,1,0:T(8,128)(2,1)S(1)} copy-done((bf16[1,9,128,128]{3,2,1,0:T(8,128)(2,1)S(1)}, bf16[1,9,128,128]{3,2,1,0:T(8,128)(2,1)}, u32[]{:S(2)}) %copy-start.3) | copy-done | bytes 294936
  4.7 0.0 copy-start.4
  4.7 0.7 copy-done.4
  5.4 71.1 %shard_map.68 = (f32[256,512]{1,0:T(8,128)S(1)}, f32[256,512]{1,0:T(8,128)S(1)}) custom-call(f32[256,512]{1,0:T(8,128)S(1)} %copy-done, f32[256,512]{1,0:T(8,128)S(1)} %copy-done.1, bf16[1,9,128,128]{3,2,1,0:T(8,128)(2,1)S(1)} %copy-done.3, s32[4,8]{1,0:T(4,128)S(1)} %copy-done.4, bf16[256,1024]{1,0:T(8,128)(2,1)S(1)} %copy-done.2), custom_call_target="tpu_custom_call" | custom-call | flops 1207959552 | bytes 1048576 | tf_op jit(solution)/shard_map/pallas_call | solution.py:285
  76.5 0.8 %copy.9 = f32[256,512]{1,0:T(8,128)} copy(f32[256,512]{1,0:T(8,128)S(1)} %get-tuple-element.4) | data formatting | bytes 1048576
  77.3 0.8 %copy.10 = f32[256,512]{1,0:T(8,128)} copy(f32[256,512]{1,0:T(8,128)S(1)} %get-tuple-element.5) | data formatting | bytes 1048576
Async XLA Ops:
  0.6 1.0 %copy-start = (f32[256,512]{1,0:T(8,128)S(1)}, f32[256,512]{1,0:T(8,128)}, u32[]{:S(2)}) copy-start(f32[256,512]{1,0:T(8,128)} %right_ref.1) | copy-start | bytes 1572868
  1.7 1.0 %copy-start.1 = (f32[256,512]{1,0:T(8,128)S(1)}, f32[256,512]{1,0:T(8,128)}, u32[]{:S(2)}) copy-start(f32[256,512]{1,0:T(8,128)} %initial_ref.1) | copy-start | bytes 1572868
  2.7 1.0 %copy-start.2 = (bf16[256,1024]{1,0:T(8,128)(2,1)S(1)}, bf16[256,1024]{1,0:T(8,128)(2,1)}, u32[]{:S(2)}) copy-start(bf16[256,1024]{1,0:T(8,128)(2,1)} %cov_ref.1) | copy-start | bytes 1572868
  3.8 1.0 %copy-start.3 = (bf16[1,9,128,128]{3,2,1,0:T(8,128)(2,1)S(1)}, bf16[1,9,128,128]{3,2,1,0:T(8,128)(2,1)}, u32[]{:S(2)}) copy-start(bf16[1,9,128,128]{3,2,1,0:T(8,128)(2,1)} %blocks_ref.1) | copy-start | bytes 884740
  4.7 0.7 copy-start.4

commit v2 on v1

--- a/solution.py
+++ b/solution.py
@@ -29,11 +29,11 @@
 def kernel(
     regions,
     peers,
-    right_ref,
+    right_hbm,
     initial_ref,
     blocks_ref,
     places_ref,
-    cov_ref,
+    cov_hbm,
     solution_ref,
     residual_ref,
     matrix,
@@ -53,12 +53,28 @@
     near_recv,
     far_send,
     far_recv,
+    right_mem,
+    cov_mem,
+    load,
+    built,
+    first,
+    offset,
+    arrived,
+    given,
+    back,
+    residual,
 ):
+    right_load = pltpu.make_async_copy(right_hbm, right_mem, load.at[0])
+    cov_load = pltpu.make_async_copy(cov_hbm, cov_mem, load.at[1])
+    right_load.start()
+    cov_load.start()
+    right_ref, cov_ref = right_mem, cov_mem
     hours, sites = right_ref.shape
     own_rows, slots, tile, _ = blocks_ref.shape
     rows = places_ref.shape[0]
     half = rows // 2
     edge = half * tile
+    turns = ITERS + 1
     chips = peers // CORES
     region = lax.axis_index("region")
     peer = lax.axis_index("tm")
@@ -130,31 +146,30 @@
                 place = chips - 1 + step
                 await_into(self.view(other), self.send.at[place], self.recv.at[place])
 
-    def send_halo(turn, value):
-        field = wide.at[turn]
-        field[1] = value[:, 0:edge].astype(jnp.bfloat16)
-        field[2] = value[:, edge:sites].astype(jnp.bfloat16)
-        if turn == 0:
-            pl.semaphore_wait(barrier, peers + regions - 2)
-            matrix_gather.begin()
-        start(
-            field.at[2],
-            field.at[0],
-            halo_send.at[turn, 0],
-            halo_recv.at[turn, 0],
-            (region_at(1), peer),
+    lower = peer < peers // 2
+    behind = (region_at(-1), peer)
+    ahead = (region_at(1), peer)
+
+    def spot(index):
+        return pl.ds(lax.rem(index * own_rows + half, rows), own_rows)
+
+    def shift_copy(level):
+        return copy(
+            built.at[level],
+            matrix.at[level, spot(peer)],
+            halo_send.at[turns + 2 + level],
+            halo_recv.at[turns + 2 + level],
+            behind,
         )
-        start(
-            field.at[1],
-            field.at[3],
-            halo_send.at[turn, 1],
-            halo_recv.at[turn, 1],
-            (region_at(-1), peer),
+
+    matrix_gathers = [
+        Gather(
+            lambda index, level=level: matrix.at[level, spot(index)],
+            matrix_send.at[level],
+            matrix_recv.at[level],
         )
-
-    matrix_gather = Gather(
-        lambda index: matrix.at[pl.ds(index * own_rows, own_rows)], matrix_send, matrix_recv
-    )
+        for level in range(2)
+    ]
 
     def build_matrix():
         for own in range(own_rows):
@@ -171,27 +186,50 @@
                     total = total + weight * blocks_ref[own, slot].astype(jnp.float32)
                 high = total.astype(jnp.bfloat16)
                 low = (total - high.astype(jnp.float32)).astype(jnp.bfloat16)
-                across = slice(column * tile, (column + 1) * tile)
-                matrix[row, 0, :, across] = high
-                matrix[row, 1, :, across] = low
-
-    def operate(turn):
+                span = slice(column * tile, (column + 1) * tile)
+                built[0, own, :, span] = high
+                built[1, own, :, span] = low
+
+        @pl.when(jnp.logical_not(lower))
+        def _():
+            for level in range(2):
+                matrix[level, spot(peer)] = built[level]
+
+    def begin():
+        start(first, wide.at[0, 1], halo_send.at[turns], halo_recv.at[turns], behind)
+
+        @pl.when(lower)
+        def _():
+            for level in range(2):
+                shift_copy(level).start()
+
+        start(offset, arrived, halo_send.at[turns + 1], halo_recv.at[turns + 1], behind)
+        for level in range(2):
+
+            @pl.when(lower)
+            def _():
+                shift_copy(level).wait_recv()
+
+            matrix_gathers[level].begin()
+        for gather in matrix_gathers:
+            gather.forward()
+
+    def operate(turn, meanwhile):
+        field = wide.at[turn]
         if turn == 0:
-            matrix_gather.forward()
-            matrix_gather.finish()
-        field = wide.at[turn]
+            await_into(field.at[1], halo_send.at[turns], halo_recv.at[turns])
+            for gather in matrix_gathers:
+                gather.finish()
         gathers = []
-        for side in range(2):
-            landed = field.at[3 * side]
-            await_into(landed, halo_send.at[turn, side], halo_recv.at[turn, side])
+        for side in (1, 0):
             spatial = jnp.zeros((hours, edge), jnp.float32)
             for level in range(2):
                 for piece in range(2):
                     part = matrix[
-                        side * half : (side + 1) * half, level, :, piece * edge : (piece + 1) * edge
+                        level, side * half : (side + 1) * half, :, piece * edge : (piece + 1) * edge
                     ]
                     spatial = spatial + lax.dot_general(
-                        field[2 * side + piece],
+                        field[piece],
                         part.reshape(edge, edge),
                         NT,
                         preferred_element_type=jnp.float32,
@@ -203,21 +241,29 @@
                 field_recv.at[turn, side],
             )
             gather.begin()
-            gathers.append(gather)
-        for gather in gathers:
+            gathers.append((side, gather))
+        meanwhile()
+        for side, gather in gathers:
             gather.forward()
-        for side, gather in enumerate(gathers):
+        for side, gather in gathers:
             gather.finish()
-            columns = slice(side * edge, (side + 1) * edge)
             temporal = jnp.dot(
                 cov_ref[...], gathered[turn, side], preferred_element_type=jnp.float32
-            )
-            yield columns, temporal.astype(jnp.bfloat16).astype(jnp.float32)
+            ).astype(jnp.bfloat16)
+            if side == 1:
+                given[turn] = temporal
+                start(given.at[turn], back.at[turn], halo_send.at[turn], halo_recv.at[turn], ahead)
+            yield side, temporal.astype(jnp.float32)
+
+    def returned(turn):
+        await_into(back.at[turn], halo_send.at[turn], halo_recv.at[turn])
+        return back[turn].astype(jnp.float32)
 
     def reduce(turn, parts):
-        count = len(parts) * 8
-        for place, part in enumerate(parts):
-            near[turn, peer, place * 8 : (place + 1) * 8, :] = part
+        count = 8
+        packed = [jnp.sum(part, axis=0, keepdims=True) for part in parts]
+        packed.append(jnp.zeros((count - len(parts), 128), jnp.float32))
+        near[turn, peer] = jnp.concatenate(packed, axis=0)
         own = near.at[turn, peer, 0:count]
         for step in range(1, peers):
             start(own, own, near_send.at[turn, step], near_recv.at[turn, step], (region, peer_at(step)))
@@ -238,35 +284,86 @@
                 far_recv.at[turn, step],
             )
         whole = jnp.sum(far[turn, :, 0:count, :], axis=0)
-        return [total_of(whole[place * 8 : (place + 1) * 8]) for place in range(len(parts))]
+        return [total_of(whole[place : place + 1]) for place in range(len(parts))]
 
     build_matrix()
-    send_halo(0, initial_ref[...])
-    for columns, temporal in operate(0):
-        direction[:, columns] = right_ref[:, columns] - (initial_ref[:, columns] + temporal)
-    residual_ref[...] = direction[...]
+    first[...] = initial_ref[:, 0:edge].astype(jnp.bfloat16)
+    wide[0, 0] = initial_ref[:, edge:sites].astype(jnp.bfloat16)
+    right_load.wait()
+    offset[...] = right_ref[:, 0:edge] - initial_ref[:, 0:edge]
+    pl.semaphore_wait(barrier, peers + regions - 2)
+    begin()
     solution_ref[...] = initial_ref[...]
+    for side, temporal in operate(0, cov_load.wait):
+        if side == 1:
+            await_into(arrived, halo_send.at[turns + 1], halo_recv.at[turns + 1])
+            direction[2] = arrived[...] - temporal
+        else:
+            direction[1] = right_ref[:, edge:sites] - (initial_ref[:, edge:sites] + temporal)
+    residual[1:3] = direction[1:3]
+
+    def late_start():
+        value = right_ref[:, 0:edge] - (initial_ref[:, 0:edge] + returned(0))
+        direction[0] = value
+        residual[0] = value
+
+    def step(part, size, picture):
+        moved = direction[part]
+        residual[part] = residual[part] - size * picture
+        if part < 2:
+            span = slice(part * edge, (part + 1) * edge)
+            solution_ref[:, span] = solution_ref[:, span] + size * moved
+
+    def turn_to(part, ratio):
+        direction[part] = residual[part] + ratio * direction[part]
+
+    def late_step(turn, size):
+        step(0, size, direction[0] + returned(turn + 1))
+
     norm = None
+    meanwhile = late_start
     for turn in range(ITERS):
-        send_halo(turn + 1, direction[...])
-        for columns, temporal in operate(turn + 1):
-            image[:, columns] = direction[:, columns] + temporal
-        parts = [fold(direction[...] * image[...])]
+        wide[turn + 1, 0] = direction[1].astype(jnp.bfloat16)
+        wide[turn + 1, 1] = direction[2].astype(jnp.bfloat16)
+        for side, temporal in operate(turn + 1, meanwhile):
+            image[side] = direction[side + 1] + temporal
+
+        def inner(left, right):
+            return fold(left[0] * right[0]) + fold(left[1] * right[1])
+
+        moved, rest, picture = direction[1:3], residual[1:3], image[...]
+        parts = [inner(moved, picture)]
         if turn + 1 < ITERS:
-            parts.append(fold(residual_ref[...] * image[...]))
-            parts.append(fold(image[...] * image[...]))
+            parts.append(inner(rest, picture))
+            parts.append(inner(picture, picture))
         if turn == 0:
-            parts.append(fold(residual_ref[...] * residual_ref[...]))
+            parts.append(inner(rest, rest))
         sums = reduce(turn, parts)
         if turn == 0:
             norm = sums[-1]
-        step_size = norm / sums[0]
-        solution_ref[...] = solution_ref[...] + step_size * direction[...]
-        residual_ref[...] = residual_ref[...] - step_size * image[...]
+        size = norm / sums[0]
+        step(1, size, image[0])
         if turn + 1 < ITERS:
-            later = norm - 2.0 * step_size * sums[1] + step_size * step_size * sums[2]
-            direction[...] = residual_ref[...] + later / norm * direction[...]
+            step(2, size, image[1])
+            later = norm - 2.0 * size * sums[1] + size * size * sums[2]
+            ratio = later / norm
+            turn_to(1, ratio)
+            turn_to(2, ratio)
             norm = later
+
+            def meanwhile(turn=turn, size=size, ratio=ratio):
+                late_step(turn, size)
+                turn_to(0, ratio)
+        else:
+            late_step(turn, size)
+    residual_ref[:, 0:edge] = residual[0]
+    residual_ref[:, edge:sites] = residual[1]
+
+    @pl.when(lower)
+    def _():
+        for level in range(2):
+            shift_copy(level).wait_send()
+
     for made in pending:
         made.wait_send()
 
@@ -276,8 +373,10 @@
     rows = neighbour_blocks.shape[0]
     tile = blocks.shape[2]
     turns = ITERS + 1
+    edge = sites // 2
     dma = pltpu.SemaphoreType.DMA
     vmem = pl.BlockSpec(memory_space=pltpu.VMEM)
+    hbm = pl.BlockSpec(memory_space=pltpu.HBM)
     out = jax.ShapeDtypeStruct((hours, sites), jnp.float32)
     width = 2 * sites
     held = 4 * (rows * tile) ** 2 + 4 * turns * sites * hours * (peers // 2 + 1) + 24 * hours * sites
@@ -285,29 +384,39 @@
     return pl.pallas_call(
         functools.partial(kernel, regions, peers),
         out_shape=(out, out),
-        in_specs=[vmem, vmem, vmem, pl.BlockSpec(memory_space=pltpu.SMEM), vmem],
+        in_specs=[hbm, vmem, vmem, pl.BlockSpec(memory_space=pltpu.SMEM), hbm],
         out_specs=(vmem, vmem),
         scratch_shapes=[
-            pltpu.VMEM((rows, 2, tile, rows * tile), jnp.bfloat16),
-            pltpu.VMEM((turns, 4, hours, sites // 2), jnp.bfloat16),
+            pltpu.VMEM((2, rows, tile, rows * tile), jnp.bfloat16),
+            pltpu.VMEM((turns, 2, hours, edge), jnp.bfloat16),
             pltpu.VMEM((turns, 2, hours * peers, sites // 2), jnp.bfloat16),
-            pltpu.VMEM((hours, sites), jnp.float32),
-            pltpu.VMEM((hours, sites), jnp.float32),
-            pltpu.VMEM((ITERS, peers, 32, 128), jnp.float32),
-            pltpu.VMEM((ITERS, regions, 32, 128), jnp.float32),
-            dma((turns, 2)),
-            dma((turns, 2)),
-            dma((peers - 1,)),
-            dma((peers - 1,)),
+            pltpu.VMEM((3, hours, edge), jnp.float32),
+            pltpu.VMEM((2, hours, edge), jnp.float32),
+            pltpu.VMEM((ITERS, peers, 8, 128), jnp.float32),
+            pltpu.VMEM((ITERS, regions, 8, 128), jnp.float32),
+            dma((turns + 4,)),
+            dma((turns + 4,)),
+            dma((2, peers - 1)),
+            dma((2, peers - 1)),
             dma((turns, 2, peers - 1)),
             dma((turns, 2, peers - 1)),
             dma((ITERS, peers)),
             dma((ITERS, peers)),
             dma((ITERS, regions)),
             dma((ITERS, regions)),
+            pltpu.VMEM(right_side.shape, right_side.dtype),
+            pltpu.VMEM(temporal_cov.shape, temporal_cov.dtype),
+            dma((2,)),
+            pltpu.VMEM((2, blocks.shape[0], tile, rows * tile), jnp.bfloat16),
+            pltpu.VMEM((hours, edge), jnp.bfloat16),
+            pltpu.VMEM((hours, edge), jnp.float32),
+            pltpu.VMEM((hours, edge), jnp.float32),
+            pltpu.VMEM((turns, hours, edge), jnp.bfloat16),
+            pltpu.VMEM((turns, hours, edge), jnp.bfloat16),
+            pltpu.VMEM((3, hours, edge), jnp.float32),
         ],
         compiler_params=pltpu.CompilerParams(
-            collective_id=0, has_side_effects=True, vmem_limit_bytes=min(3 * held, 58 << 20)
+            collective_id=0, has_side_effects=True, vmem_limit_bytes=58 << 20
         ),
         cost_estimate=pl.CostEstimate(flops=flops, bytes_accessed=4 * hours * width, transcendentals=0),
     )(right_side, initial, blocks, neighbour_blocks, temporal_cov)

time: 78.4 us -> 68.2 us (0.87)
  Pallas kernels: 71.1 us -> 64.6 us
  local copies, waits for them, and re-layouts: 6.35 us -> 2.72 us
    pallas_call x1, Pallas kernels: 71.1 us -> 64.6 us  [local(): pl.pallas_call(functools.partial(kernel, regions, peers), out_shape=(out,...]
    unnamed x12 -> x4, local copies, waits for them, and re-layouts: 6.35 us -> 2.72 us
where the time goes in v2:
time: 68.2 us; the launch traced here: 68 us
  Pallas kernels  64.6 us (95%)
  local copies, waits for them, and re-layouts  2.72 us (4%)
    pallas_call x1, Pallas kernels, local(): pl.pallas_call(functools.partial(kernel, regions, peers), out_shape=(out,...  64.6 us
    unnamed x4, local copies, waits for them, and re-layouts  2.72 us

profile of v2, /device:TPU:0, one launch (start us, length us, event | category | flops | bytes accessed | tf_op | source)
XLA Modules:
  0.0 68.0 jit_solution(5045986302697521533)
XLA Ops:
  0.6 64.6 %shard_map.68 = (f32[256,512]{1,0:T(8,128)}, f32[256,512]{1,0:T(8,128)}) custom-call(f32[256,512]{1,0:T(8,128)} %right_hbm.1, f32[256,512]{1,0:T(8,128)} %initial_ref.1, bf16[1,9,128,128]{3,2,1,0:T(8,128)(2,1)} %blocks_ref.1, s32[4,8]{1,0:T(4,128)} %places_ref.1, bf16[256,1024]{1,0:T(8,128)(2,1)} %cov_hbm.1), custom_call_target="tpu_custom_call" | custom-call | flops 1207959552 | bytes 1048576 | tf_op jit(solution)/shard_map/pallas_call | solution.py:384
  65.3 0.0 copy-start
  65.3 1.9 %copy.9 = f32[256,512]{1,0:T(8,128)} copy(f32[256,512]{1,0:T(8,128)} %get-tuple-element.4) | data formatting | bytes 1048576
  67.2 0.0 copy-done
  67.2 0.8 %copy.10 = f32[256,512]{1,0:T(8,128)} copy(f32[256,512]{1,0:T(8,128)S(1)} %copy-done) | data formatting | bytes 1048576
Async XLA Ops:
  65.3 1.9 %copy-start = (f32[256,512]{1,0:T(8,128)S(1)}, f32[256,512]{1,0:T(8,128)}, u32[]{:S(2)}) copy-start(f32[256,512]{1,0:T(8,128)} %get-tuple-element.5) | copy-start | bytes 1572868

commit v3 on v2

--- a/solution.py
+++ b/solution.py
@@ -168,7 +168,7 @@
             matrix_send.at[level],
             matrix_recv.at[level],
         )
-        for level in range(2)
+        for level in range(4)
     ]
 
     def build_matrix():
@@ -186,33 +186,40 @@
                     total = total + weight * blocks_ref[own, slot].astype(jnp.float32)
                 high = total.astype(jnp.bfloat16)
                 low = (total - high.astype(jnp.float32)).astype(jnp.bfloat16)
-                span = slice(column * tile, (column + 1) * tile)
-                built[0, own, :, span] = high
-                built[1, own, :, span] = low
+                piece, place = divmod(column, half)
+                span = slice(place * tile, (place + 1) * tile)
+                built[piece, own, :, span] = high
+                built[2 + piece, own, :, span] = low
 
         @pl.when(jnp.logical_not(lower))
         def _():
-            for level in range(2):
+            for level in range(4):
                 matrix[level, spot(peer)] = built[level]
 
     def begin():
-        start(first, wide.at[0, 1], halo_send.at[turns], halo_recv.at[turns], behind)
-
         @pl.when(lower)
         def _():
             for level in range(2):
                 shift_copy(level).start()
 
-        start(offset, arrived, halo_send.at[turns + 1], halo_recv.at[turns + 1], behind)
-        for level in range(2):
+        start(first, wide.at[0, 1], halo_send.at[turns], halo_recv.at[turns], behind)
+
+        @pl.when(lower)
+        def _():
+            for level in range(2, 4):
+                shift_copy(level).start()
+
+
+        for level in range(4):
 
             @pl.when(lower)
             def _():
                 shift_copy(level).wait_recv()
 
             matrix_gathers[level].begin()
-        for gather in matrix_gathers:
-            gather.forward()
+            if level > 0:
+                matrix_gathers[level - 1].forward()
+        matrix_gathers[3].forward()
 
     def operate(turn, meanwhile):
         field = wide.at[turn]
@@ -221,13 +228,13 @@
             for gather in matrix_gathers:
                 gather.finish()
         gathers = []
+        if turn == 0:
+            start(offset, arrived, halo_send.at[turns + 1], halo_recv.at[turns + 1], behind)
         for side in (1, 0):
             spatial = jnp.zeros((hours, edge), jnp.float32)
             for level in range(2):
                 for piece in range(2):
-                    part = matrix[
-                        level, side * half : (side + 1) * half, :, piece * edge : (piece + 1) * edge
-                    ]
+                    part = matrix[2 * level + piece, side * half : (side + 1) * half]
                     spatial = spatial + lax.dot_general(
                         field[piece],
                         part.reshape(edge, edge),
@@ -361,7 +368,7 @@
 
     @pl.when(lower)
     def _():
-        for level in range(2):
+        for level in range(4):
             shift_copy(level).wait_send()
 
     for made in pending:
@@ -387,17 +394,17 @@
         in_specs=[hbm, vmem, vmem, pl.BlockSpec(memory_space=pltpu.SMEM), hbm],
         out_specs=(vmem, vmem),
         scratch_shapes=[
-            pltpu.VMEM((2, rows, tile, rows * tile), jnp.bfloat16),
+            pltpu.VMEM((4, rows, tile, edge), jnp.bfloat16),
             pltpu.VMEM((turns, 2, hours, edge), jnp.bfloat16),
             pltpu.VMEM((turns, 2, hours * peers, sites // 2), jnp.bfloat16),
             pltpu.VMEM((3, hours, edge), jnp.float32),
             pltpu.VMEM((2, hours, edge), jnp.float32),
             pltpu.VMEM((ITERS, peers, 8, 128), jnp.float32),
             pltpu.VMEM((ITERS, regions, 8, 128), jnp.float32),
-            dma((turns + 4,)),
-            dma((turns + 4,)),
-            dma((2, peers - 1)),
-            dma((2, peers - 1)),
+            dma((turns + 6,)),
+            dma((turns + 6,)),
+            dma((4, peers - 1)),
+            dma((4, peers - 1)),
             dma((turns, 2, peers - 1)),
             dma((turns, 2, peers - 1)),
             dma((ITERS, peers)),
@@ -407,7 +414,7 @@
             pltpu.VMEM(right_side.shape, right_side.dtype),
             pltpu.VMEM(temporal_cov.shape, temporal_cov.dtype),
             dma((2,)),
-            pltpu.VMEM((2, blocks.shape[0], tile, rows * tile), jnp.bfloat16),
+            pltpu.VMEM((4, blocks.shape[0], tile, edge), jnp.bfloat16),
             pltpu.VMEM((hours, edge), jnp.bfloat16),
             pltpu.VMEM((hours, edge), jnp.float32),
             pltpu.VMEM((hours, edge), jnp.float32),

time: 68.2 us -> 66.6 us (0.977)
  Pallas kernels: 64.6 us -> 63.1 us
    pallas_call x1, Pallas kernels: 64.6 us -> 63.1 us  [local(): pl.pallas_call(functools.partial(kernel, regions, peers), out_shape=(out,...]
where the time goes in v3:
time: 66.6 us; the launch traced here: 66.5 us
  Pallas kernels  63.1 us (95%)
  local copies, waits for them, and re-layouts  2.72 us (4%)
    pallas_call x1, Pallas kernels, local(): pl.pallas_call(functools.partial(kernel, regions, peers), out_shape=(out,...  63.1 us
    unnamed x4, local copies, waits for them, and re-layouts  2.72 us

profile of v3, /device:TPU:0, one launch (start us, length us, event | category | flops | bytes accessed | tf_op | source)
XLA Modules:
  0.0 66.5 jit_solution(6283559479085917399)
XLA Ops:
  0.6 63.1 %shard_map.68 = (f32[256,512]{1,0:T(8,128)}, f32[256,512]{1,0:T(8,128)}) custom-call(f32[256,512]{1,0:T(8,128)} %right_hbm.1, f32[256,512]{1,0:T(8,128)} %initial_ref.1, bf16[1,9,128,128]{3,2,1,0:T(8,128)(2,1)} %blocks_ref.1, s32[4,8]{1,0:T(4,128)} %places_ref.1, bf16[256,1024]{1,0:T(8,128)(2,1)} %cov_hbm.1), custom_call_target="tpu_custom_call" | custom-call | flops 1207959552 | bytes 1048576 | tf_op jit(solution)/shard_map/pallas_call | solution.py:391
  63.7 0.0 copy-start
  63.7 1.9 %copy.9 = f32[256,512]{1,0:T(8,128)} copy(f32[256,512]{1,0:T(8,128)} %get-tuple-element.4) | data formatting | bytes 1048576
  65.7 0.0 copy-done
  65.7 0.8 %copy.10 = f32[256,512]{1,0:T(8,128)} copy(f32[256,512]{1,0:T(8,128)S(1)} %copy-done) | data formatting | bytes 1048576
Async XLA Ops:
  63.7 1.9 %copy-start = (f32[256,512]{1,0:T(8,128)S(1)}, f32[256,512]{1,0:T(8,128)}, u32[]{:S(2)}) copy-start(f32[256,512]{1,0:T(8,128)} %get-tuple-element.5) | copy-start | bytes 1572868
